TPU v7x, 32 devices: a whole 2x2x4 slice. The times are simulated.
32 devices in a mesh: grid: 8 (over z, x), orb: 4 (over y, core).
Axes of the slice: x: 2, y: 2, z: 4, core: 2. Of those that a mesh axis runs over, the one named last changes fastest.
Arguments:
- collocation: bfloat16 [3072, 8192], P('orb', 'grid'), may hold values from -6 to 6
- amplitude: bfloat16 [3072, 1536], P('orb'), may hold values from -0.109375 to 0.109375
- occupied: bfloat16 [1536, 8192], P('orb', 'grid'), may hold values from -6 to 6
- quadrature: bfloat16 [8192, 1536], P('grid'), may hold values from -6 to 6
- pair_list: int32 [8, 4, 48], P('grid', 'orb'), may hold values from 0 to 47, as said below
- pair_count: int32 [8, 4], P('grid', 'orb'), may hold values from 12 to 48, as said below
Outputs:
- residual: float32 [1536, 3072], P('grid', 'orb')
Inputs may be any that keep to these rules, and one draw needn't show every extreme that they name: `pair_list`: within each device's list the entries are distinct. `pair_count`: some device has all 48 pairs live.
All inputs are finite; a program needn't handle non-finite values.
Results may differ from a plain program's by a relative error of at most 0.0045.
Values may be sent and summed in bfloat16 or wider, within the bound.
A program may use at most 64 MiB of HBM per device.

v0:
```python
import math

import jax
import jax.numpy as jnp
from jax import lax
from jax.sharding import PartitionSpec as P

BLK = 128
OB_DEV = 6
GB_DEV = 8


def shards(collocation, amplitude, occupied, quadrature, pair_list, pair_count):
    orb_rows, grid_cols = collocation.shape
    rank = amplitude.shape[1]
    n_grid = lax.axis_size("grid")
    total_grid = grid_cols * n_grid
    slots = pair_list.shape[-1]
    listed = pair_list.reshape(slots)
    numbers = jnp.arange(slots, dtype=jnp.int32)
    live = numbers < pair_count.reshape(())
    hits = jnp.logical_and(listed[:, None] == numbers[None, :], live[:, None])
    screen = jnp.any(hits, axis=0).astype(jnp.bfloat16).reshape(GB_DEV, OB_DEV)
    masked = (collocation.reshape(OB_DEV, BLK, GB_DEV, BLK) * screen.T[:, None, :, None]).reshape(
        orb_rows, grid_cols
    )
    projected = lax.psum_scatter(
        lax.dot_general(
            amplitude, masked, (((0,), (0,)), ((), ())), preferred_element_type=jnp.float32
        ),
        "orb",
        scatter_dimension=0,
        tiled=True,
    )
    occupied_full = occupied.astype(jnp.float32)
    hadamard = (projected * occupied_full).astype(jnp.bfloat16)
    partial_ladder = jnp.dot(hadamard, quadrature, preferred_element_type=jnp.float32)
    ladder = (lax.psum(partial_ladder, "grid") * (1.0 / math.sqrt(total_grid))).astype(jnp.bfloat16)
    spread = lax.dot_general(
        ladder, quadrature, (((1,), (1,)), ((), ())), preferred_element_type=jnp.float32
    )
    back = (occupied_full * spread * (1.0 / math.sqrt(rank))).astype(jnp.bfloat16)
    gathered = lax.all_gather(back, "orb", axis=0, tiled=True)
    share = rank // n_grid
    summed = lax.psum(
        lax.dot_general(
            gathered, collocation, (((1,), (1,)), ((), ())), preferred_element_type=jnp.float32
        ),
        "grid",
    )
    result = lax.dynamic_slice_in_dim(summed, lax.axis_index("grid") * share, share, 0)
    return result * (1.0 / math.sqrt(total_grid))


def solution(mesh):
    return jax.shard_map(
        shards,
        mesh=mesh,
        in_specs=(
            P("orb", "grid"),
            P("orb", None),
            P("orb", "grid"),
            P("grid", None),
            P("grid", "orb", None),
            P("grid", "orb"),
        ),
        out_specs=P("grid", "orb"),
        check_vma=False,
    )
```

profile of v0, /device:TPU:0, one launch (start us, length us, event | category | flops | bytes accessed | tf_op | source)
XLA Modules:
  0.0 408.0 jit_solution(17339549369115358609)
XLA Ops:
  6.5 0.0 copy-start
  6.5 0.0 reduce-scatter.2.cloned.1.call-start
  7.4 0.9 fusion.8
  8.3 0.1 reshape.17
  8.3 0.1 copy.8
  8.4 0.3 mul.38
  8.7 7.5 %convolution_bitcast_fusion = f32[1536,1024]{1,0:T(8,128)} fusion(bf16[768,1536]{1,0:T(8,128)(2,1)} %param.7, bf16[768,1024]{1,0:T(8,128)(2,1)} %param.6, bf16[96,8,8,128]{3,2,1,0:T(8,128)(2,1)S(1)} %bitcast.16), kind=kOutput, calls=%fused_computation | convolution fusion | flops 2416705536 | bytes 11796480 | tf_op jit(solution)/shard_map/dot_general | solution.py:28
  16.2 0.0 reduce-scatter.2.cloned.1.call-update
  16.2 0.0 all-reduce.3.cloned.1.call-start
  16.3 61.1 %reduce-scatter.2.cloned.1.call-done = f32[384,1024]{1,0:T(8,128)} async-done(((f32[1536,1024]{1,0:T(8,128)}), f32[384,1024]{1,0:T(8,128)}) %reduce-scatter.2.cloned.1.call-update) | async-done | bytes 1572880 | tf_op jit(solution)/shard_map/reduce_scatter | solution.py:27
  77.4 0.0 copy-done
  77.4 4.4 %fusion.5 = f32[384,1536]{1,0:T(8,128)} fusion(bf16[1024,1536]{1,0:T(8,128)(2,1)S(1)} %copy-done, f32[384,1024]{1,0:T(8,128)} %reduce-scatter.2.cloned.1.call-done, bf16[384,1024]{1,0:T(8,128)(2,1)} %param.8), kind=kOutput, calls=%fused_computation.10 | convolution fusion | flops 1209139200 | bytes 7864320 | tf_op jit(solution)/shard_map/dot_general | solution.py:37
  81.8 0.0 all-reduce.3.cloned.1.call-update
  81.8 0.0 all-gather.2.cloned.1.call-start
  81.9 108.9 %all-reduce.3.cloned.1.call-done = f32[384,1536]{1,0:T(8,128)} async-done(((f32[384,1536]{1,0:T(8,128)}), f32[384,1536]{1,0:T(8,128)}) %all-reduce.3.cloned.1.call-update) | async-done | bytes 2359312 | tf_op jit(solution)/shard_map/psum | solution.py:38
  190.7 4.2 %fusion.2 = bf16[384,1024]{1,0:T(8,128)(2,1)} fusion(bf16[384,1024]{1,0:T(8,128)(2,1)} %param.8, bf16[1024,1536]{1,0:T(8,128)(2,1)S(1)} %copy-done, f32[384,1536]{1,0:T(8,128)} %all-reduce.3.cloned.1.call-done), kind=kOutput, calls=%fused_computation.6 | convolution fusion | flops 1210712064 | bytes 7077888 | tf_op jit(solution)/shard_map/dot_general | solution.py:39
  194.9 0.0 all-gather.2.cloned.1.call-update
  194.9 0.0 all-reduce.5.cloned.1.call-start
  194.9 27.7 %all-gather.2.cloned.1.call-done = bf16[1536,1024]{1,0:T(8,128)(2,1)} async-done(((bf16[384,1024]{1,0:T(8,128)(2,1)}), bf16[1536,1024]{1,0:T(8,128)(2,1)}) %all-gather.2.cloned.1.call-update) | async-done | bytes 3145744 | tf_op jit(solution)/shard_map/all_gather | solution.py:43
  222.6 7.1 %fusion.10 = f32[1536,768]{1,0:T(8,128)} fusion(bf16[1536,1024]{1,0:T(8,128)(2,1)} %all-gather.2.cloned.1.call-done, bf16[768,1024]{1,0:T(8,128)(2,1)} %param.6), kind=kOutput, calls=%fused_computation.17 | convolution fusion | flops 2415919104 | bytes 9437184 | tf_op jit(solution)/shard_map/dot_general | solution.py:46
  229.8 0.0 all-reduce.5.cloned.1.call-update
  229.8 169.8 %all-reduce.5.cloned.1.call-done = f32[1536,768]{1,0:T(8,128)} async-done(((f32[1536,768]{1,0:T(8,128)}), f32[1536,768]{1,0:T(8,128)}) %all-reduce.5.cloned.1.call-update) | async-done | bytes 4718608 | tf_op jit(solution)/shard_map/psum | solution.py:45
  399.6 1.9 dynamic-slice_multiply_fusion
  (2 shorter events, 0.0 us)
Async XLA Ops:
  6.5 70.9 %copy-start = (bf16[1024,1536]{1,0:T(8,128)(2,1)S(1)}, bf16[1024,1536]{1,0:T(8,128)(2,1)}, u32[]{:S(2)}) copy-start(bf16[1024,1536]{1,0:T(8,128)(2,1)} %param.9) | copy-start | bytes 9437188
  6.5 70.9 %reduce-scatter.2.cloned.1.call-start = ((), (), s32[]{:S(2)}) async-start(), calls=%async_computation.1 | async-start | bytes 7864320 | tf_op jit(solution)/shard_map/reduce_scatter | solution.py:27
  16.2 174.5 %all-reduce.3.cloned.1.call-start = ((), (), s32[]{:S(2)}) async-start(), calls=%async_computation.2 | async-start | bytes 4718592 | tf_op jit(solution)/shard_map/psum | solution.py:38
  81.8 140.8 %all-gather.2.cloned.1.call-start = ((), (), s32[]{:S(2)}) async-start(), calls=%async_computation.3 | async-start | bytes 3932160 | tf_op jit(solution)/shard_map/all_gather | solution.py:43
  194.9 204.7 %all-reduce.5.cloned.1.call-start = ((), (), s32[]{:S(2)}) async-start(), calls=%async_computation.4 | async-start | bytes 9437184 | tf_op jit(solution)/shard_map/psum | solution.py:45
Sparse Core Ops, SparseCore 0:
  16.3 61.0 reduce-scatter.1
  81.9 108.7 all-reduce.2
  195.0 27.5 all-gather.1
  229.9 169.6 all-reduce.4
where the time goes:
time: 408 us
  waiting for transfers between devices  368 us (90%)
  matrix products  23.1 us (6%)
  between operations  14 us (3%)
    psum x1, waiting for transfers between devices, shards(): lax.psum(lax.dot_general(gathered, collocation, (((1,), (1,)), ((), ())),...  170 us
    psum x1, waiting for transfers between devices, shards(): lax.psum(partial_ladder, 'grid') * (1.0 / math.sqrt(total_grid))  109 us
    reduce_scatter x1, waiting for transfers between devices, shards(): lax.psum_scatter(lax.dot_general(amplitude, masked, (((0,), (0,)), ((), (...  61.1 us
    all_gather x1, waiting for transfers between devices, shards(): gathered = lax.all_gather(back, 'orb', axis=0, tiled=True)  27.7 us
  transfers between devices with their start and end apart: 4, of which 4 were waited for; matrix products, arithmetic and copies ran while one was open for 0% of the time, Pallas kernels for 0%

commit v1 on v0

v1 whole, which is shorter than its diff:
```python
import functools
import math

import jax
import jax.numpy as jnp
from jax import lax
from jax.experimental import pallas as pl
from jax.experimental.pallas import tpu as pltpu
from jax.sharding import PartitionSpec as P

BLK = 128
OB_DEV = 6
GB_DEV = 8
CORES = 2
UNIT = 48
MESH = pl.DeviceIdType.MESH
F32 = jnp.float32
BF16 = jnp.bfloat16


def kernel(
    n_grid, n_orb, n_x, chunks, total_grid,
    coll_ref, amp_ref, occ_ref, quad_ref, list_ref, count_ref, out_ref,
    masked, other1, own1, recv1, ysend, yrecv, had, lpart, lxsend, lxrecv, lzsend, lzrecv,
    ladder, ladder_flat, back, rpart, rxsend, rxrecv, rzsend, rzrecv,
    c1_s, c1_r, y1_s, y1_r, lx_s, lx_r, lz_s, lz_r, gz_s, gz_r, gx_s, gx_r,
    by_s, by_r, bc_s, bc_r, rx_s, rx_r, rz_s, rz_r,
):
    n_y = n_orb // CORES
    n_z = n_grid // n_x
    a_dev, pts = coll_ref.shape
    rank = quad_ref.shape[1]
    rows_orb = rank // n_orb
    rows_dev = rank // n_grid
    unit = rows_dev // chunks
    wide = n_x * unit
    cols = rank // n_z
    inv_grid = 1.0 / math.sqrt(total_grid)
    inv_rank = 1.0 / math.sqrt(rank)

    g, o = lax.axis_index("grid"), lax.axis_index("orb")
    z, x = g // n_x, g % n_x
    y, core = o // CORES, o % CORES

    core_peer = (g, y * CORES + (1 - core))
    ys = [(y + d) % n_y for d in range(1, n_y)]
    xs = [(x + d) % n_x for d in range(1, n_x)]
    zs = [(z + d) % n_z for d in range(1, n_z)]
    y_peers = [(g, q * CORES + core) for q in ys]
    x_peers = [(z * n_x + q, o) for q in xs]
    z_peers = [(q * n_x + x, o) for q in zs]

    barrier = pltpu.get_barrier_semaphore()
    peers = [core_peer] + y_peers + x_peers + z_peers
    for peer in peers:
        pl.semaphore_signal(barrier, inc=1, device_id=peer, device_id_type=MESH)

    def remote(src, dst, send, recv, peer):
        return pltpu.make_async_remote_copy(
            src_ref=src, dst_ref=dst, send_sem=send, recv_sem=recv, device_id=peer, device_id_type=MESH
        )

    def core_sum(c):
        return remote(other1.at[c], recv1.at[c], c1_s.at[c], c1_r.at[c], core_peer)

    def y_sum(c, d):
        return remote(ysend.at[c, d], yrecv.at[c, d], y1_s.at[c, d], y1_r.at[c, d], y_peers[d])

    def lx_sum(c, d):
        return remote(lxsend.at[c, xs[d]], lxrecv.at[c, d], lx_s.at[c, d], lx_r.at[c, d], x_peers[d])

    def lz_sum(c, d):
        return remote(lzsend.at[c, zs[d]], lzrecv.at[c, d], lz_s.at[c, d], lz_r.at[c, d], z_peers[d])

    def lz_gather(c, d):
        mine = ladder.at[c, x, z]
        return remote(mine, mine, gz_s.at[c, d], gz_r.at[c, d], z_peers[d])

    def lx_gather(c, d):
        mine = ladder.at[c, x]
        return remote(mine, mine, gx_s.at[c, d], gx_r.at[c, d], x_peers[d])

    def by_gather(c, d):
        mine = back.at[c, o]
        return remote(mine, mine, by_s.at[c, d], by_r.at[c, d], y_peers[d])

    def bc_gather(c, d):
        piece = back.at[c, ((y + n_y - d) % n_y) * CORES + core]
        return remote(piece, piece, bc_s.at[c, d], bc_r.at[c, d], core_peer)

    def rx_sum(c, d):
        return remote(rxsend.at[c, xs[d]], rxrecv.at[c, d], rx_s.at[c, d], rx_r.at[c, d], x_peers[d])

    def rz_sum(c, d):
        return remote(rzsend.at[c, zs[d]], rzrecv.at[c, d], rz_s.at[c, d], rz_r.at[c, d], z_peers[d])

    slots = list_ref.shape[1]
    blocks = lax.broadcasted_iota(jnp.int32, (slots, slots), 0)
    places = lax.broadcasted_iota(jnp.int32, (slots, slots), 1)
    live = jnp.logical_and(list_ref[...] == blocks, places < count_ref[...])
    screen = jnp.max(jnp.where(live, 1.0, 0.0), axis=1, keepdims=True)
    for gb in range(GB_DEV):
        for ob in range(OB_DEV):
            number = gb * OB_DEV + ob
            part = (slice(ob * BLK, (ob + 1) * BLK), slice(gb * BLK, (gb + 1) * BLK))
            keep = jnp.broadcast_to(screen[number : number + 1, :], (BLK, BLK))
            masked[part] = (coll_ref[part].astype(F32) * keep).astype(BF16)

    tile = 256
    tiles = pts // tile

    def project(which, dest):
        def step(i, carry):
            q = i // tiles
            at = pl.ds(pl.multiple_of((i % tiles) * tile, tile), tile)
            index = q * CORES + which
            if len(amp_ref.shape) == 3:
                factor = amp_ref[index]
            else:
                factor = amp_ref[:, pl.ds(pl.multiple_of(index * rows_orb, BLK), rows_orb)]
            value = lax.dot_general(
                factor, masked[:, at], (((0,), (0,)), ((), ())), preferred_element_type=F32
            )
            for c in range(chunks):
                for xi in range(n_x):
                    first = xi * rows_dev + c * unit
                    dest[c, q, xi, :, at] = value[first : first + unit]
            return carry

        lax.fori_loop(0, n_y * tiles, step, 0)

    def stage_b(c):
        core_sum(c).wait_recv()
        for d in range(n_y - 1):
            ysend[c, d] = (own1[c, ys[d]] + recv1[c, ys[d]]).astype(BF16)
            y_sum(c, d).start()

    def occ_rows(c):
        return jnp.concatenate(
            [occ_ref[xi * rows_dev + c * unit : xi * rows_dev + (c + 1) * unit, :] for xi in range(n_x)], axis=0
        ).astype(F32)

    def stage_d(c):
        for d in range(n_y - 1):
            y_sum(c, d).wait_recv()
        value = own1[c, y] + recv1[c, y]
        for d in range(n_y - 1):
            value = value + yrecv[c, d].astype(F32)
        had[...] = (value.reshape(wide, pts) * occ_rows(c)).astype(BF16)
        for j in range(n_z):
            value = jnp.dot(had[...], quad_ref[:, j * cols : (j + 1) * cols], preferred_element_type=F32)
            value = value.reshape(n_x, unit, cols)
            lpart[c, :, j] = value
            lxsend[c, :, j] = value.astype(BF16)
        for d in range(n_x - 1):
            lx_sum(c, d).start()

    def stage_e(c):
        for d in range(n_x - 1):
            lx_sum(c, d).wait_recv()
        value = lpart[c, x]
        for d in range(n_x - 1):
            value = value + lxrecv[c, d].astype(F32)
        lzsend[c] = value.astype(BF16)
        for d in range(n_z - 1):
            lz_sum(c, d).start()

    def stage_f(c):
        value = lpart[c, x, z]
        for d in range(n_x - 1):
            value = value + lxrecv[c, d, z].astype(F32)
        for d in range(n_z - 1):
            lz_sum(c, d).wait_recv()
            value = value + lzrecv[c, d].astype(F32)
        ladder[c, x, z] = (value * inv_grid).astype(BF16)
        for d in range(n_z - 1):
            lz_gather(c, d).start()

    def stage_g(c):
        for d in range(n_z - 1):
            lz_gather(c, d).wait_recv()
        for d in range(n_x - 1):
            lx_gather(c, d).start()

    def stage_h(c):
        for d in range(n_x - 1):
            lx_gather(c, d).wait_recv()
        for j in range(n_z):
            ladder_flat[:, j * cols : (j + 1) * cols] = ladder[c, :, j].reshape(wide, cols)
        for i in range(tiles):
            at = slice(i * tile, (i + 1) * tile)
            spread = lax.dot_general(
                ladder_flat[...], quad_ref[at, :], (((1,), (1,)), ((), ())), preferred_element_type=F32
            )
            held = jnp.concatenate(
                [
                    occ_ref[xi * rows_dev + c * unit : xi * rows_dev + (c + 1) * unit, at]
                    for xi in range(n_x)
                ],
                axis=0,
            ).astype(F32)
            back[c, o, :, at] = (held * spread * inv_rank).astype(BF16)
        for d in range(n_y - 1):
            by_gather(c, d).start()
        bc_gather(c, 0).start()

    def stage_i(c):
        for d in range(n_y - 1):
            by_gather(c, d).wait_recv()
            bc_gather(c, d + 1).start()

    def stage_j(c):
        for d in range(n_y):
            bc_gather(c, d).wait_recv()
        def step(i, carry):
            at = pl.ds(pl.multiple_of(i * tile, tile), tile)
            value = lax.dot_general(
                back[c].reshape(n_orb * wide, pts), coll_ref[at, :], (((1,), (1,)), ((), ())),
                preferred_element_type=F32,
            ).reshape(n_orb, n_x, unit, tile)
            for xi in range(n_x):
                rpart[c, xi, :, :, at] = value[:, xi]
                rxsend[c, xi, :, :, at] = value[:, xi].astype(BF16)
            return carry

        lax.fori_loop(0, a_dev // tile, step, 0)
        for d in range(n_x - 1):
            rx_sum(c, d).start()

    def stage_k(c):
        for d in range(n_x - 1):
            rx_sum(c, d).wait_recv()
        value = rpart[c, x]
        for d in range(n_x - 1):
            value = value + rxrecv[c, d].astype(F32)
        rzsend[c] = value.astype(BF16)
        for d in range(n_z - 1):
            rz_sum(c, d).start()

    def stage_l(c):
        value = rpart[c, x, z]
        for d in range(n_x - 1):
            value = value + rxrecv[c, d, z].astype(F32)
        for d in range(n_z - 1):
            rz_sum(c, d).wait_recv()
            value = value + rzrecv[c, d].astype(F32)
        out_ref[c * unit : (c + 1) * unit, :] = value * inv_grid

    project(1 - core, other1)
    pl.semaphore_wait(barrier, len(peers))
    for c in range(chunks):
        core_sum(c).start()
    project(core, own1)

    stages = [stage_b, stage_d, stage_e, stage_f, stage_g, stage_h, stage_i, stage_j, stage_k, stage_l]
    for t in range(len(stages) + chunks - 1):
        for c in range(chunks):
            if 0 <= t - c < len(stages):
                stages[t - c](c)

    for c in range(chunks):
        core_sum(c).wait_send()
        for d in range(n_y - 1):
            y_sum(c, d).wait_send()
            by_gather(c, d).wait_send()
        for d in range(n_y):
            bc_gather(c, d).wait_send()
        for d in range(n_x - 1):
            lx_sum(c, d).wait_send()
            lx_gather(c, d).wait_send()
            rx_sum(c, d).wait_send()
        for d in range(n_z - 1):
            lz_sum(c, d).wait_send()
            lz_gather(c, d).wait_send()
            rz_sum(c, d).wait_send()


def shards(n_grid, n_orb, collocation, amplitude, occupied, quadrature, pair_list, pair_count):
    a_dev, pts = collocation.shape
    rank = amplitude.shape[1]
    n_x = math.isqrt(n_grid // 2)
    n_z = n_grid // n_x
    n_y = n_orb // CORES
    assert n_z == n_orb and n_x * n_z == n_grid
    rows_dev = rank // n_grid
    chunks = rows_dev // UNIT
    wide = n_x * UNIT
    cols = rank // n_z
    if (rank // n_orb) % BLK:
        amplitude = amplitude.reshape(a_dev, n_orb, rank // n_orb).transpose(1, 0, 2)
    vmem = pltpu.VMEM

    def sems(n):
        return [pltpu.SemaphoreType.DMA((chunks, n))] * 2

    one = [pltpu.SemaphoreType.DMA((chunks,))] * 2
    return pl.pallas_call(
        functools.partial(kernel, n_grid, n_orb, n_x, chunks, pts * n_grid),
        out_shape=jax.ShapeDtypeStruct((rows_dev, a_dev), F32),
        in_specs=[pl.BlockSpec(memory_space=vmem)] * 6,
        out_specs=pl.BlockSpec(memory_space=vmem),
        scratch_shapes=[
            vmem((a_dev, pts), BF16),
            vmem((chunks, n_y, n_x, UNIT, pts), F32),
            vmem((chunks, n_y, n_x, UNIT, pts), F32),
            vmem((chunks, n_y, n_x, UNIT, pts), F32),
            vmem((chunks, n_y - 1, n_x, UNIT, pts), BF16),
            vmem((chunks, n_y - 1, n_x, UNIT, pts), BF16),
            vmem((wide, pts), BF16),
            vmem((chunks, n_x, n_z, UNIT, cols), F32),
            vmem((chunks, n_x, n_z, UNIT, cols), BF16),
            vmem((chunks, n_x - 1, n_z, UNIT, cols), BF16),
            vmem((chunks, n_z, UNIT, cols), BF16),
            vmem((chunks, n_z - 1, UNIT, cols), BF16),
            vmem((chunks, n_x, n_z, UNIT, cols), BF16),
            vmem((wide, rank), BF16),
            vmem((chunks, n_orb, wide, pts), BF16),
            vmem((chunks, n_x, n_orb, UNIT, a_dev), F32),
            vmem((chunks, n_x, n_orb, UNIT, a_dev), BF16),
            vmem((chunks, n_x - 1, n_orb, UNIT, a_dev), BF16),
            vmem((chunks, n_orb, UNIT, a_dev), BF16),
            vmem((chunks, n_z - 1, UNIT, a_dev), BF16),
            *one,
            *sems(n_y - 1),
            *sems(n_x - 1),
            *sems(n_z - 1),
            *sems(n_z - 1),
            *sems(n_x - 1),
            *sems(n_y - 1),
            *sems(n_y),
            *sems(n_x - 1),
            *sems(n_z - 1),
        ],
        compiler_params=pltpu.CompilerParams(
            collective_id=0, has_side_effects=True, vmem_limit_bytes=60 * 2**20
        ),
        cost_estimate=pl.CostEstimate(
            flops=2 * a_dev * rank * pts * 2 + 4 * (rank // n_orb) * pts * rank,
            bytes_accessed=10_000_000,
            transcendentals=0,
        ),
    )(
        collocation, amplitude, occupied, quadrature,
        pair_list.reshape(1, -1), pair_count.reshape(1, 1),
    )


def solution(mesh):
    return jax.shard_map(
        functools.partial(shards, mesh.shape["grid"], mesh.shape["orb"]),
        mesh=mesh,
        in_specs=(
            P("orb", "grid"),
            P("orb", None),
            P("orb", "grid"),
            P("grid", None),
            P("grid", "orb", None),
            P("grid", "orb"),
        ),
        out_specs=P("grid", "orb"),
        check_vma=False,
    )
```

time: 408 us -> 94.8 us (0.23)
  waiting for transfers between devices: 368 us -> 0 us
  Pallas kernels: 0 us -> 92.1 us
  matrix products: 23.1 us -> 0 us
  between operations: 14 us -> 0.66 us
    psum x2 -> x0, waiting for transfers between devices: 279 us -> none  [the longest x1 170 us: shards(): lax.psum(lax.dot_general(gathered, collocation, (((1,), (1,)), ((), ())),...]
    pallas_call x0 -> x1, Pallas kernels: none -> 92.1 us  [shards(): pl.pallas_call(functools.partial(kernel, n_grid, n_orb, n_x, chunks, pts...]
    reduce_scatter x1 -> x0, waiting for transfers between devices: 61.1 us -> none  [shards(): lax.psum_scatter(lax.dot_general(amplitude, masked, (((0,), (0,)), ((), (...]
    all_gather x1 -> x0, waiting for transfers between devices: 27.7 us -> none  [shards(): gathered = lax.all_gather(back, 'orb', axis=0, tiled=True)]
    dot_general x4 -> x0, matrix products: 23.1 us -> none  [the longest x1 7.45 us: shards(): lax.dot_general(amplitude, masked, (((0,), (0,)), ((), ())), preferred_el...]
  transfers between devices with their start and end apart: 4 -> 0, of which waited for: 4 -> 0; matrix products, arithmetic and copies ran while one was open for 0% -> 0% of each run, Pallas kernels for 0% -> 0%
where the time goes in v1:
time: 94.8 us; the launch traced here: 94.6 us
  Pallas kernels  92.1 us (97%)
  local copies, waits for them, and re-layouts  1.92 us (2%)
    pallas_call x1, Pallas kernels, shards(): pl.pallas_call(functools.partial(kernel, n_grid, n_orb, n_x, chunks, pts...  92.1 us
    unnamed x1, local copies, waits for them, and re-layouts  1.92 us

profile of v1, /device:TPU:0, one launch (start us, length us, event | category | flops | bytes accessed | tf_op | source)
XLA Modules:
  0.0 94.6 jit_solution(653926277942227467)
XLA Ops:
  0.7 92.1 %shard_map.64 = f32[192,768]{1,0:T(8,128)} custom-call(bf16[768,1024]{1,0:T(8,128)(2,1)} %coll_ref.1, bf16[768,1536]{1,0:T(8,128)(2,1)} %amp_ref.1, bf16[384,1024]{1,0:T(8,128)(2,1)} %occ_ref.1, bf16[1024,1536]{1,0:T(8,128)(2,1)} %quad_ref.1, s32[1,48]{1,0:T(1,128)} %bitcast.1, s32[1,1]{1,0:T(1,128)S(6)} %copy.8.count_ref), custom_call_target="tpu_custom_call" | custom-call | flops 7247757312 | bytes 10000000 | tf_op jit(solution)/shard_map/pallas_call | solution.py:297
  92.7 1.9 %copy.9 = f32[192,768]{1,0:T(8,128)} copy(f32[192,768]{1,0:T(8,128)} %shard_map.64) | data formatting | bytes 1179648

commit v2 on v1

--- a/solution.py
+++ b/solution.py
@@ -20,7 +20,8 @@
 
 def kernel(
     n_grid, n_orb, n_x, chunks, total_grid,
-    coll_ref, amp_ref, occ_ref, quad_ref, list_ref, count_ref, out_ref,
+    coll_ref, amp_ref, occ_hbm, quad_hbm, list_ref, count_ref, out_ref,
+    occ_ref, quad_ref, load_sem,
     masked, other1, own1, recv1, ysend, yrecv, had, lpart, lxsend, lxrecv, lzsend, lzrecv,
     ladder, ladder_flat, back, rpart, rxsend, rxrecv, rzsend, rzrecv,
     c1_s, c1_r, y1_s, y1_r, lx_s, lx_r, lz_s, lz_r, gz_s, gz_r, gx_s, gx_r,
@@ -29,7 +30,7 @@
     n_y = n_orb // CORES
     n_z = n_grid // n_x
     a_dev, pts = coll_ref.shape
-    rank = quad_ref.shape[1]
+    rank = quad_hbm.shape[1]
     rows_orb = rank // n_orb
     rows_dev = rank // n_grid
     unit = rows_dev // chunks
@@ -93,6 +94,13 @@
 
     def rz_sum(c, d):
         return remote(rzsend.at[c, zs[d]], rzrecv.at[c, d], rz_s.at[c, d], rz_r.at[c, d], z_peers[d])
+
+    loads = [
+        pltpu.make_async_copy(occ_hbm, occ_ref, load_sem.at[0]),
+        pltpu.make_async_copy(quad_hbm, quad_ref, load_sem.at[1]),
+    ]
+    for load in loads:
+        load.start()
 
     slots = list_ref.shape[1]
     blocks = lax.broadcasted_iota(jnp.int32, (slots, slots), 0)
@@ -251,6 +259,8 @@
     for c in range(chunks):
         core_sum(c).start()
     project(core, own1)
+    for load in loads:
+        load.wait()
 
     stages = [stage_b, stage_d, stage_e, stage_f, stage_g, stage_h, stage_i, stage_j, stage_k, stage_l]
     for t in range(len(stages) + chunks - 1):
@@ -297,9 +307,12 @@
     return pl.pallas_call(
         functools.partial(kernel, n_grid, n_orb, n_x, chunks, pts * n_grid),
         out_shape=jax.ShapeDtypeStruct((rows_dev, a_dev), F32),
-        in_specs=[pl.BlockSpec(memory_space=vmem)] * 6,
+        in_specs=[pl.BlockSpec(memory_space=m) for m in (vmem, vmem, pl.ANY, pl.ANY, vmem, vmem)],
         out_specs=pl.BlockSpec(memory_space=vmem),
         scratch_shapes=[
+            vmem(occupied.shape, BF16),
+            vmem(quadrature.shape, BF16),
+            pltpu.SemaphoreType.DMA((2,)),
             vmem((a_dev, pts), BF16),
             vmem((chunks, n_y, n_x, UNIT, pts), F32),
             vmem((chunks, n_y, n_x, UNIT, pts), F32),

time: 94.8 us -> 93.7 us (0.988)
  Pallas kernels: 92.1 us -> 91 us
    pallas_call x1, Pallas kernels: 92.1 us -> 91 us  [shards(): pl.pallas_call(functools.partial(kernel, n_grid, n_orb, n_x, chunks, pts...]
where the time goes in v2:
time: 93.7 us; the launch traced here: 93.5 us
  Pallas kernels  91 us (97%)
  local copies, waits for them, and re-layouts  1.92 us (2%)
    pallas_call x1, Pallas kernels, shards(): pl.pallas_call(functools.partial(kernel, n_grid, n_orb, n_x, chunks, pts...  91 us
    unnamed x1, local copies, waits for them, and re-layouts  1.92 us

profile of v2, /device:TPU:0, one launch (start us, length us, event | category | flops | bytes accessed | tf_op | source)
XLA Modules:
  0.0 93.5 jit_solution(5051315794639000218)
XLA Ops:
  0.7 91.0 %shard_map.64 = f32[192,768]{1,0:T(8,128)} custom-call(bf16[768,1024]{1,0:T(8,128)(2,1)} %coll_ref.1, bf16[768,1536]{1,0:T(8,128)(2,1)} %amp_ref.1, bf16[384,1024]{1,0:T(8,128)(2,1)} %occ_hbm.1, bf16[1024,1536]{1,0:T(8,128)(2,1)} %quad_hbm.1, s32[1,48]{1,0:T(1,128)} %bitcast.1, s32[1,1]{1,0:T(1,128)S(6)} %copy.8.count_ref), custom_call_target="tpu_custom_call" | custom-call | flops 7247757312 | bytes 10000000 | tf_op jit(solution)/shard_map/pallas_call | solution.py:307
  91.6 1.9 %copy.9 = f32[192,768]{1,0:T(8,128)} copy(f32[192,768]{1,0:T(8,128)} %shard_map.64) | data formatting | bytes 1179648

commit v3 on v2

--- a/solution.py
+++ b/solution.py
@@ -61,8 +61,9 @@
             src_ref=src, dst_ref=dst, send_sem=send, recv_sem=recv, device_id=peer, device_id_type=MESH
         )
 
-    def core_sum(c):
-        return remote(other1.at[c], recv1.at[c], c1_s.at[c], c1_r.at[c], core_peer)
+    def core_sum(c, d):
+        q = (y + 1 + d) % n_y
+        return remote(other1.at[c, q], recv1.at[c, q], c1_s.at[c, d], c1_r.at[c, d], core_peer)
 
     def y_sum(c, d):
         return remote(ysend.at[c, d], yrecv.at[c, d], y1_s.at[c, d], y1_r.at[c, d], y_peers[d])
@@ -117,9 +118,9 @@
     tile = 256
     tiles = pts // tile
 
-    def project(which, dest):
+    def project(which, dest, first_block, last_block):
         def step(i, carry):
-            q = i // tiles
+            q = (y + 1 + i // tiles) % n_y
             at = pl.ds(pl.multiple_of((i % tiles) * tile, tile), tile)
             index = q * CORES + which
             if len(amp_ref.shape) == 3:
@@ -135,11 +136,11 @@
                     dest[c, q, xi, :, at] = value[first : first + unit]
             return carry
 
-        lax.fori_loop(0, n_y * tiles, step, 0)
+        lax.fori_loop(first_block * tiles, last_block * tiles, step, 0)
 
     def stage_b(c):
-        core_sum(c).wait_recv()
-        for d in range(n_y - 1):
+        for d in range(n_y - 1):
+            core_sum(c, d).wait_recv()
             ysend[c, d] = (own1[c, ys[d]] + recv1[c, ys[d]]).astype(BF16)
             y_sum(c, d).start()
 
@@ -151,6 +152,7 @@
     def stage_d(c):
         for d in range(n_y - 1):
             y_sum(c, d).wait_recv()
+        core_sum(c, n_y - 1).wait_recv()
         value = own1[c, y] + recv1[c, y]
         for d in range(n_y - 1):
             value = value + yrecv[c, d].astype(F32)
@@ -254,22 +256,30 @@
             value = value + rzrecv[c, d].astype(F32)
         out_ref[c * unit : (c + 1) * unit, :] = value * inv_grid
 
-    project(1 - core, other1)
+    project(1 - core, other1, 0, n_y - 1)
     pl.semaphore_wait(barrier, len(peers))
     for c in range(chunks):
-        core_sum(c).start()
-    project(core, own1)
+        for d in range(n_y - 1):
+            core_sum(c, d).start()
+    project(core, own1, 0, n_y - 1)
+    for c in range(chunks):
+        stage_b(c)
+    project(1 - core, other1, n_y - 1, n_y)
+    for c in range(chunks):
+        core_sum(c, n_y - 1).start()
+    project(core, own1, n_y - 1, n_y)
     for load in loads:
         load.wait()
 
-    stages = [stage_b, stage_d, stage_e, stage_f, stage_g, stage_h, stage_i, stage_j, stage_k, stage_l]
-    for t in range(len(stages) + chunks - 1):
-        for c in range(chunks):
-            if 0 <= t - c < len(stages):
-                stages[t - c](c)
+    stages = [stage_d, stage_e, stage_f, stage_g, stage_h, stage_i, stage_j, stage_k, stage_l]
+    times = (2, 4, 6, 7, 9, 11, 12, 14, 16)
+    order = sorted((times[s] + 2 * c, c, s) for s in range(len(stages)) for c in range(chunks))
+    for _, c, s in order:
+        stages[s](c)
 
     for c in range(chunks):
-        core_sum(c).wait_send()
+        for d in range(n_y):
+            core_sum(c, d).wait_send()
         for d in range(n_y - 1):
             y_sum(c, d).wait_send()
             by_gather(c, d).wait_send()
@@ -303,7 +313,6 @@
     def sems(n):
         return [pltpu.SemaphoreType.DMA((chunks, n))] * 2
 
-    one = [pltpu.SemaphoreType.DMA((chunks,))] * 2
     return pl.pallas_call(
         functools.partial(kernel, n_grid, n_orb, n_x, chunks, pts * n_grid),
         out_shape=jax.ShapeDtypeStruct((rows_dev, a_dev), F32),
@@ -333,7 +342,7 @@
             vmem((chunks, n_x - 1, n_orb, UNIT, a_dev), BF16),
             vmem((chunks, n_orb, UNIT, a_dev), BF16),
             vmem((chunks, n_z - 1, UNIT, a_dev), BF16),
-            *one,
+            *sems(n_y),
             *sems(n_y - 1),
             *sems(n_x - 1),
             *sems(n_z - 1),

time: 93.7 us -> 89.1 us (0.951)
  Pallas kernels: 91 us -> 86.3 us
    pallas_call x1, Pallas kernels: 91 us -> 86.3 us  [shards(): pl.pallas_call(functools.partial(kernel, n_grid, n_orb, n_x, chunks, pts...]
where the time goes in v3:
time: 89.1 us; the launch traced here: 88.9 us
  Pallas kernels  86.3 us (97%)
  local copies, waits for them, and re-layouts  1.92 us (2%)
    pallas_call x1, Pallas kernels, shards(): pl.pallas_call(functools.partial(kernel, n_grid, n_orb, n_x, chunks, pts...  86.3 us
    unnamed x1, local copies, waits for them, and re-layouts  1.92 us

profile of v3, /device:TPU:0, one launch (start us, length us, event | category | flops | bytes accessed | tf_op | source)
XLA Modules:
  0.0 88.9 jit_solution(15283336364427100918)
XLA Ops:
  0.7 86.3 %shard_map.64 = f32[192,768]{1,0:T(8,128)} custom-call(bf16[768,1024]{1,0:T(8,128)(2,1)} %coll_ref.1, bf16[768,1536]{1,0:T(8,128)(2,1)} %amp_ref.1, bf16[384,1024]{1,0:T(8,128)(2,1)} %occ_hbm.1, bf16[1024,1536]{1,0:T(8,128)(2,1)} %quad_hbm.1, s32[1,48]{1,0:T(1,128)} %bitcast.1, s32[1,1]{1,0:T(1,128)S(6)} %copy.8.count_ref), custom_call_target="tpu_custom_call" | custom-call | flops 7247757312 | bytes 10000000 | tf_op jit(solution)/shard_map/pallas_call | solution.py:316
  87.0 1.9 %copy.9 = f32[192,768]{1,0:T(8,128)} copy(f32[192,768]{1,0:T(8,128)} %shard_map.64) | data formatting | bytes 1179648
